TPU v7x, 256 devices: a whole 4x4x8 slice. The times are simulated.
256 devices in a mesh: seq: 64 (over z, x, core), chan: 4 (over y).
Axes of the slice: x: 4, y: 4, z: 8, core: 2. Of those that a mesh axis runs over, the one named last changes fastest.
Arguments:
- tokens: bfloat16 [24576, 4096], P('seq'), as said below
- norm_gain: float32 [4096], replicated, may hold values from 0.1 to 1.9
- in_weight: bfloat16 [4096, 3, 4096], P('seq', None, 'chan'), may hold values from -0.09375 to 0.09375
- short_taps: float32 [3, 7, 4096], P(None, None, 'chan'), may hold values from -2 to 2
- decay_rates: float32 [16, 4096], P(None, 'chan'), as said below
- residues: float32 [16, 4096], P(None, 'chan'), may hold values from -3 to 3
- bypass: float32 [4096], P('chan'), may hold values from -4 to 4
- out_weight: bfloat16 [4096, 4096], P('chan'), may hold values from -0.09375 to 0.09375
Outputs:
- block_out: bfloat16 [24576, 4096], P('seq', 'chan')
Inputs may be any that keep to these rules, and one draw needn't show every extreme that they name: `tokens`: residual stream activations. `decay_rates`: positive decay rates of the modes.
All inputs are finite; a program needn't handle non-finite values.
Results may differ from a plain program's by a relative error of at most 0.029.
Values may be sent and summed in bfloat16 or wider, within the bound.
No kernel may reach another device: no remote copies, remote signals or barrier semaphores. Data moves between devices by JAX's collectives and lax.ppermute only.
A program may use at most 256 MiB of HBM per device.

v0:
```python
import jax
import jax.numpy as jnp
from jax import lax
from jax.sharding import PartitionSpec as P

SHORT = 7
BLOCK = 64


def from_behind(block, axis, distance):
    devices = range(lax.axis_size(axis))
    route = [(i - distance, i) for i in devices if i - distance in devices]
    return lax.ppermute(block, axis, route)


def on_device(tokens, norm_gain, in_weight, short_taps, decay_rates, residues, bypass, out_weight):
    rows_here = tokens.shape[0]
    chans_here = in_weight.shape[2]
    rim_count = SHORT - 1
    count_blocks = rows_here // BLOCK
    highest = lax.Precision.HIGHEST
    widened = tokens.astype(jnp.float32)
    square_mean = jnp.mean(widened * widened, axis=1, keepdims=True)
    normed = (widened * lax.rsqrt(square_mean + 1e-05) * norm_gain[None, :]).astype(jnp.bfloat16)
    piece = lax.all_gather(in_weight, "seq", axis=0, tiled=True)
    flat_piece = piece.reshape(piece.shape[0], 3 * chans_here)
    summed = jnp.dot(normed, flat_piece, preferred_element_type=jnp.float32)
    projected = summed.astype(jnp.bfloat16).reshape(normed.shape[0], 3, chans_here)
    rim_rows = from_behind(projected[rows_here - rim_count :], "seq", 1)
    extended = jnp.concatenate([rim_rows, projected], axis=0)
    extended_wide = extended.astype(jnp.float32)
    featured = jnp.zeros((rows_here, 3, chans_here), jnp.float32)
    for offset in range(SHORT):
        featured = (
            featured
            + short_taps[None, :, offset, :]
            * extended_wide[rim_count - offset : rim_count - offset + rows_here]
        )
    gated = (featured[:, 1, :] * featured[:, 2, :]).astype(jnp.bfloat16)
    gated_wide = gated.astype(jnp.float32)
    lags = jnp.arange(BLOCK + 1).astype(jnp.float32)
    powers = jnp.exp(-decay_rates[None, :, :] * lags[:, None, None])
    mode_gain = residues * jnp.sqrt(-jnp.expm1(-2.0 * decay_rates))
    filter_taps = jnp.sum(mode_gain[None, :, :] * powers[:BLOCK], axis=1)
    lag_index = jnp.arange(BLOCK)
    selector = (
        lag_index[:, None, None] - lag_index[None, :, None] == lag_index[None, None, :]
    ).astype(jnp.float32)
    toeplitz = jnp.einsum("tsk,kc->tsc", selector, filter_taps, precision=highest)
    entering = mode_gain[None, :, :] * powers[1:]
    leaving = jnp.flip(powers[:BLOCK], axis=0)
    decay_block = powers[BLOCK]
    blocks = gated_wide.reshape(count_blocks, BLOCK, chans_here)
    inside = jnp.einsum("tsc,isc->itc", toeplitz, blocks, precision=highest)
    block_sums = jnp.einsum("smc,isc->imc", leaving, blocks, precision=highest)

    def advance(state, block_sum):
        return (decay_block * state + block_sum, state)

    zero_state = jnp.zeros_like(decay_block)
    local_end, local_before = lax.scan(advance, zero_state, block_sums)
    device_decay = jnp.exp(-decay_rates * float(rows_here))

    def relay(turn_index, carry):
        received = from_behind(carry[1].astype(jnp.bfloat16), "seq", 1).astype(jnp.float32)
        return (received, device_decay * received + local_end)

    incoming, _ = lax.fori_loop(0, lax.axis_size("seq") - 1, relay, (zero_state, local_end))
    block_starts = (jnp.arange(count_blocks) * BLOCK).astype(jnp.float32)
    reach = jnp.exp(-decay_rates[None, :, :] * block_starts[:, None, None])
    before = local_before + reach * incoming[None, :, :]
    carried = jnp.einsum("tmc,imc->itc", entering, before, precision=highest)
    convolved = (inside + carried).reshape(rows_here, chans_here)
    modulated = (featured[:, 0, :] * (convolved + bypass[None, :] * gated_wide)).astype(
        jnp.bfloat16
    )
    terms = jnp.dot(modulated, out_weight, preferred_element_type=jnp.float32)
    block_out = lax.psum_scatter(
        terms.astype(jnp.bfloat16), "chan", scatter_dimension=1, tiled=True
    )
    return block_out


def solution(mesh):
    in_specs = (
        P("seq", None),
        P(),
        P("seq", None, "chan"),
        P(None, None, "chan"),
        P(None, "chan"),
        P(None, "chan"),
        P("chan"),
        P("chan", None),
    )
    out_specs = P("seq", "chan")
    return jax.shard_map(
        on_device, mesh=mesh, in_specs=in_specs, out_specs=out_specs, check_vma=False
    )
```

profile of v0, /device:TPU:1, one launch (start us, length us, event | category | flops | bytes accessed | tf_op | source)
XLA Modules:
  0.0 969.0 jit_solution(3641934498767897437)
XLA Ops:
  17.4 10.2 %fusion.12 = f32[64,64,1024]{2,1,0:T(8,128)} fusion(s32[64,64]{1,0:T(8,128)S(1)} %iota_subtract_fusion, f32[64,1024]{1,0:T(8,128)S(1)} %get-tuple-element.117), kind=kOutput, calls=%fused_computation.32 | convolution fusion | flops 3221487616 | bytes 17055744 | tf_op jit(solution)/shard_map/tsk,kc->tsc/dot_general | solution.py:49
  27.6 108.1 %all-gather.2.cloned.1.call-done = bf16[4096,3,1024]{2,0,1:T(8,128)(2,1)} async-done(((bf16[64,3,1024]{2,0,1:T(8,128)(2,1)}), bf16[4096,3,1024]{2,0,1:T(8,128)(2,1)}) %all-gather.2.cloned.1.call-update) | async-done | bytes 25165840 | tf_op jit(solution)/shard_map/all_gather | solution.py:25
  135.7 33.3 %copy.28 = bf16[4096,3,1024]{0,2,1:T(8,128)(2,1)} copy(bf16[4096,3,1024]{2,0,1:T(8,128)(2,1)} %all-gather.2.cloned.1.call-done) | data formatting | bytes 50331648 | tf_op jit(solution)/shard_map/all_gather | solution.py:25
  169.1 15.3 %convolution_convert_fusion.1 = bf16[384,3072]{1,0:T(8,128)(2,1)} fusion(bf16[4096,3072]{0,1:T(8,128)(2,1)} %bitcast.58, bf16[384,4096]{1,0:T(8,128)(2,1)S(1)} %copy-done.1, f32[4096]{0:T(1024)S(1)} %copy-done.3, f32[384]{0:T(512)S(1)} %add_rsqrt_fusion), kind=kOutput, calls=%fused_computation.23 | convolution fusion | flops 9671147520 | bytes 30688768 | tf_op jit(solution)/shard_map/dot_general | solution.py:27
  192.0 8.7 copy.36
  200.7 8.7 copy.39
  209.4 30.5 %copy.34 = f32[64,64,1024]{1,0,2:T(8,128)} copy(f32[64,64,1024]{2,1,0:T(8,128)} %fusion.12) | data formatting | bytes 33554432 | tf_op jit(solution)/shard_map/tsk,kc->tsc/dot_general | solution.py:49
  247.6 11.2 %fusion.3 = f32[384,3,1024]{0,2,1:T(8,128)S(1)} fusion(f32[390,3,1024]{0,2,1:T(8,128)S(1)} %maximum_convert_fusion, f32[3,1024]{1,0:T(4,128)S(1)} %get-tuple-element.130, f32[3,1024]{1,0:T(4,128)S(1)} %get-tuple-element.131, f32[3,1024]{1,0:T(4,128)S(1)} %get-tuple-element.132, f32[3,1024]{1,0:T(4,128)S(1)} %get-tuple-element.133, ...), kind=kLoop, calls=%fused_computation.10 | loop fusion | flops 15335424 | bytes 37834752 | tf_op jit(solution)/shard_map/add | solution.py:35
  264.9 10.3 %convolution_bitcast_fusion = f32[6,16,1024]{1,0,2:T(8,128)} fusion(bf16[6,64,1024]{1,0,2:T(8,128)(2,1)S(1)} %copy.33, f32[64,16,1024]{0,1,2:T(8,128)} %copy.36), kind=kOutput, calls=%fused_computation.30 | convolution fusion | flops 75497472 | bytes 5373952 | tf_op jit(solution)/shard_map/smc,isc->imc/dot_general | solution.py:55
  278.6 9.1 while.26
  287.8 474.9 %while.25 = (s32[]{:T(128)}, f32[16,1024]{1,0:T(8,128)}, bf16[16,1024]{1,0:T(8,128)(2,1)S(1)}, f32[16,1024]{1,0:T(8,128)S(1)}, f32[16,1024]{1,0:T(8,128)S(1)}, /*index=5*/s32[]{:T(128)}) while((s32[]{:T(128)}, f32[16,1024]{1,0:T(8,128)}, bf16[16,1024]{1,0:T(8,128)(2,1)S(1)}, f32[16,1024]{1,0:T(8,128)S(1)}, f32[16,1024]{1,0:T(8,128)S(1)}, ...), condition=%wide.region_5.6_spmd, body=%wide.region_4.5_spmd.sunk | while | flops 65538 | bytes 393325 | solution.py:68
  356.1 6.3 collective-permute-start
  364.1 6.3 collective-permute-start
  372.1 6.3 collective-permute-start
  380.0 6.3 collective-permute-start
  388.0 6.3 collective-permute-start
  396.0 6.3 collective-permute-start
  403.9 6.3 collective-permute-start
  411.9 6.3 collective-permute-start
  419.9 6.3 collective-permute-start
  766.4 9.7 %fusion.23 = f32[1024,6,64]{2,1,0:T(8,128)S(1)} fusion(f32[6,16,1024]{1,0,2:T(8,128)} %copy.38, f32[64,16,1024]{0,1,2:T(8,128)} %copy.39), kind=kOutput, calls=%fused_computation.60 | convolution fusion | flops 75497472 | bytes 6160384 | tf_op jit(solution)/shard_map/tmc,imc->itc/dot_general | solution.py:72
  776.2 30.9 %add_bitcast_fusion = f32[6,64,1024]{1,0,2:T(8,128)} fusion(f32[1024,6,64]{2,1,0:T(8,128)S(1)} %fusion.23, bf16[6,64,1024]{1,0,2:T(8,128)(2,1)S(1)} %copy.33, f32[64,64,1024]{1,0,2:T(8,128)} %copy.34), kind=kOutput, calls=%fused_computation.25 | convolution fusion | flops 302383104 | bytes 20709376 | tf_op jit(solution)/shard_map/tsc,isc->itc/dot_general | solution.py:54
  812.6 9.1 convolution_convert_fusion
  821.7 140.5 %reduce-scatter.2.cloned.1.call-done = bf16[384,1024]{1,0:T(8,128)(2,1)} async-done(((bf16[384,4096]{1,0:T(8,128)(2,1)}), bf16[384,1024]{1,0:T(8,128)(2,1)}) %reduce-scatter.2.cloned.1.call-update) | async-done | bytes 786448 | tf_op jit(solution)/shard_map/reduce_scatter | solution.py:78
  (237 shorter events, 471.3 us)
Async XLA Ops:
  6.5 129.2 %all-gather.2.cloned.1.call-start = ((), (), s32[]{:S(2)}) async-start(), calls=%async_computation.1 | async-start | bytes 25559040 | tf_op jit(solution)/shard_map/all_gather | solution.py:25
  7.3 954.9 %reduce-scatter.2.cloned.1.call-start = ((), (), s32[]{:S(2)}) async-start(), calls=%async_computation.2 | async-start | bytes 3932160 | tf_op jit(solution)/shard_map/reduce_scatter | solution.py:78
  185.2 58.9 %collective-permute-start.1 = (bf16[6,3,1024]{2,0,1:T(8,128)(2,1)S(1)}, bf16[6,3,1024]{2,0,1:T(8,128)(2,1)S(1)}, u32[]{:S(2)}, u32[]{:S(2)}) collective-permute-start(bf16[6,3,1024]{2,0,1:T(8,128)(2,1)S(1)} %bitcast.63), channel_id=1, source_target_pairs={{0,4},{4,8},{8,12},{12,16},{16,20},{20,24},{24,28},{28,32},{32,36}... | collective-permute-start | bytes 110600 | tf_op jit(solution)/shard_map/ppermute | solution.py:13
  356.1 7.3 collective-permute-start
  364.1 7.3 collective-permute-start
  372.1 7.3 collective-permute-start
  380.0 7.3 collective-permute-start
  388.0 7.3 collective-permute-start
  396.0 7.3 collective-permute-start
  403.9 7.3 collective-permute-start
  411.9 7.3 collective-permute-start
  419.9 7.3 collective-permute-start
  435.8 7.3 collective-permute-start
  443.8 7.3 collective-permute-start
  451.8 7.3 collective-permute-start
  459.7 7.3 collective-permute-start
  467.7 7.3 collective-permute-start
  475.7 7.3 collective-permute-start
  483.7 7.3 collective-permute-start
  491.6 7.3 collective-permute-start
  499.6 7.3 collective-permute-start
  507.6 7.3 collective-permute-start
  515.5 7.3 collective-permute-start
  523.5 7.3 collective-permute-start
  (46 other events, 571.2 us)
Sparse Core Ops, SparseCore 0:
  10.2 125.4 all-gather.1
  821.8 140.2 reduce-scatter.1
where the time goes:
time: 973 us; the launch traced here: 969 us
  starting transfers between devices  373 us (38%)
  waiting for transfers between devices  312 us (32%)
  local copies, waits for them, and re-layouts  110 us (11%)
  matrix products  85.6 us (9%)
  other arithmetic  73.3 us (8%)
  between operations  13.6 us (1%)
    ppermute x64, starting transfers between devices, from_behind(): return lax.ppermute(block, axis, route)  373 us
    reduce_scatter x1, waiting for transfers between devices, on_device(): lax.psum_scatter(terms.astype(jnp.bfloat16), 'chan', scatter_dimension=1,...  140 us
    all_gather x1, waiting for transfers between devices, on_device(): piece = lax.all_gather(in_weight, 'seq', axis=0, tiled=True)  108 us
    ppermute x64, waiting for transfers between devices, from_behind(): return lax.ppermute(block, axis, route)  63.1 us
    add x63, other arithmetic, relay(): return (received, device_decay * received + local_end)  40.3 us
    all_gather x1, local copies, waits for them, and re-layouts, on_device(): piece = lax.all_gather(in_weight, 'seq', axis=0, tiled=True)  33.3 us
    dot_general x1, matrix products, on_device(): inside = jnp.einsum('tsc,isc->itc', toeplitz, blocks, precision=highest)  30.9 us
    dot_general x1, local copies, waits for them, and re-layouts, on_device(): jnp.einsum('tsk,kc->tsc', selector, filter_taps, precision=highest)  30.5 us
  transfers between devices with their start and end apart: 66, of which 65 were waited for; matrix products, arithmetic and copies ran while one was open for 8% of the time, Pallas kernels for 0%

commit v1 on v0

v1 whole, which is shorter than its diff:
```python
import functools

import jax
import jax.numpy as jnp
from jax import lax
from jax.experimental import pallas as pl
from jax.experimental.pallas import tpu as pltpu
from jax.sharding import Mesh, PartitionSpec as P

SHORT = 7
MODES = 16
LANES = 128
UNIT = 128
HALO = 16
VMEM = 48 * 1024 * 1024
bf16, f32 = jnp.bfloat16, jnp.float32


def shift(block, axes, distance):
    count = lax.axis_size(axes)
    return lax.ppermute(block, axes, [(i, (i + distance) % count) for i in range(count)])


def from_behind(block, axes, distance):
    count = lax.axis_size(axes)
    return lax.ppermute(block, axes, [(i, i + distance) for i in range(count - distance)])


def params():
    return pltpu.CompilerParams(vmem_limit_bytes=VMEM)


def norm_kernel(core_ref, own_ref, other_ref, halo_ref, gain_ref, out_ref):
    gain = gain_ref[...]

    def put(rows, src):
        wide = src.astype(f32)
        mean = jnp.mean(wide * wide, axis=1, keepdims=True)
        out_ref[rows, :] = (wide * lax.rsqrt(mean + 1e-05) * gain).astype(bf16)

    put(pl.ds(0, HALO), halo_ref[...])
    count = own_ref.shape[0]
    step = 64

    def body(i, _):
        core = core_ref[0]
        at = pl.multiple_of(i * step, step)
        own_at = pl.multiple_of(HALO + core * count + i * step, HALO)
        other_at = pl.multiple_of(HALO + (1 - core) * count + i * step, HALO)
        put(pl.ds(own_at, step), own_ref[pl.ds(at, step), :])
        put(pl.ds(other_at, step), other_ref[pl.ds(at, step), :])
        return 0

    lax.fori_loop(0, count // step, body, 0)


def norm(core, own, other, halo, gain):
    rows, width = own.shape
    whole = pl.BlockSpec(memory_space=pltpu.VMEM)
    return pl.pallas_call(
        norm_kernel,
        out_shape=jax.ShapeDtypeStruct((HALO + 2 * rows, width), bf16),
        in_specs=[pl.BlockSpec(memory_space=pltpu.SMEM)] + [whole] * 4,
        out_specs=whole,
        compiler_params=params(),
        name="norm",
    )(core, own, other, halo, gain.reshape(1, width))


def project_kernel(counts, has_acc, offs_ref, *refs):
    total = sum(counts)
    cols, refs = refs[:total], refs[total:]
    pieces, refs = refs[: len(counts)], refs[len(counts) :]
    out_ref = refs[-1]
    left = jnp.concatenate([c[...] for c in cols], axis=1)
    right = jnp.concatenate(
        [p[...].reshape(n * UNIT, p.shape[-1]) for p, n in zip(pieces, counts)], axis=0
    )
    got = jnp.dot(left, right, preferred_element_type=f32)
    if has_acc:
        got = got + refs[0][0]
    out_ref[0] = got


def project(normed, acc, pieces, places):
    rows = normed.shape[0]
    streams, width = pieces[0].shape[1], pieces[0].shape[-1]
    counts = tuple(p.shape[0] for p in pieces)
    total = sum(counts)
    offs = jnp.stack([jnp.asarray(p, jnp.int32) for p in places])
    assert offs.shape == (total,)
    in_specs = [
        pl.BlockSpec((rows, UNIT), functools.partial(lambda u, j, offs: (0, offs[u]), u))
        for u in range(total)
    ]
    in_specs += [
        pl.BlockSpec((n, 1, UNIT, width), lambda j, offs: (0, j, 0, 0)) for n in counts
    ]
    args = [normed] * total + list(pieces)
    out_spec = pl.BlockSpec((1, rows, width), lambda j, offs: (j, 0, 0))
    aliases = {}
    if acc is not None:
        in_specs.append(out_spec)
        aliases = {1 + len(args): 0}
        args.append(acc)
    flops = 2 * rows * total * UNIT * streams * width
    return pl.pallas_call(
        functools.partial(project_kernel, counts, acc is not None),
        grid_spec=pltpu.PrefetchScalarGridSpec(
            num_scalar_prefetch=1, grid=(streams,), in_specs=in_specs, out_specs=out_spec
        ),
        out_shape=jax.ShapeDtypeStruct((streams, rows, width), f32),
        input_output_aliases=aliases,
        compiler_params=params(),
        cost_estimate=pl.CostEstimate(
            flops=flops, bytes_accessed=rows * streams * width * 8, transcendentals=0
        ),
        name="project",
    )(offs, *args)


def join_kernel(count, *refs):
    for u in range(count):
        refs[-1][u] = refs[u][0]


def join(pieces, after=()):
    whole = pl.BlockSpec(memory_space=pltpu.VMEM)
    return pl.pallas_call(
        functools.partial(join_kernel, len(pieces)),
        out_shape=jax.ShapeDtypeStruct((len(pieces),) + pieces[0].shape[1:], bf16),
        in_specs=[whole] * len(pieces) + [pl.BlockSpec(memory_space=pl.ANY)] * len(after),
        out_specs=whole,
        compiler_params=params(),
        name="join",
    )(*pieces, *after)


def project_all_kernel(core_ref, left_ref, right_ref, out_ref):
    out_ref[...] = jnp.dot(left_ref[...], right_ref[0], preferred_element_type=f32)


def project_all(core, normed, weight, width):
    rows, deep = normed.shape
    block = 256
    per_core = width // block
    return pl.pallas_call(
        project_all_kernel,
        grid_spec=pltpu.PrefetchScalarGridSpec(
            num_scalar_prefetch=1,
            grid=(per_core,),
            in_specs=[
                pl.BlockSpec((rows, deep), lambda j, core: (0, 0)),
                pl.BlockSpec((1, deep, block), lambda j, core: (0, 0, core[0] * per_core + j)),
            ],
            out_specs=pl.BlockSpec((rows, block), lambda j, core: (0, j)),
        ),
        out_shape=jax.ShapeDtypeStruct((rows, width), f32),
        compiler_params=params(),
        cost_estimate=pl.CostEstimate(
            flops=2 * rows * deep * width, bytes_accessed=rows * deep * 2, transcendentals=0
        ),
        name="project_all",
    )(core, normed, weight)


def spread(wide_ref, at, depth, half, tile, val):
    rows = pl.ds(at * 8 + half * 4 + tile, depth, stride=8)
    wide_ref[rows, :] = val.astype(bf16).astype(f32)


def convolve_short(wide_ref, taps_ref, j, base, step):
    reach = step + SHORT - 1
    rows = pl.ds(pl.multiple_of((base + HALO - (SHORT - 1)) * 8, 8), reach * 8)
    x = wide_ref[rows, :].reshape(reach, 8, LANES)
    total = taps_ref[j, 0][None] * x[SHORT - 1 : SHORT - 1 + step]
    for i in range(1, SHORT):
        total = total + taps_ref[j, i][None] * x[SHORT - 1 - i : SHORT - 1 - i + step]
    return total


def gate_kernel(rows, a_ref, b_ref, taps_ref, decay_ref, reach_ref, g_ref, e0_ref, e_ref, wide_ref):
    depth = rows + HALO
    for j in range(2):
        for half in range(2):
            for tile in range(4):
                src = (a_ref, b_ref)[tile // 2]
                col = (tile % 2) * LANES
                val = src[j, half * rows : half * rows + depth, col : col + LANES]
                spread(wide_ref, j * depth, depth, half, tile, val)
    step = 8

    def body(i, state):
        at = i * step
        one = convolve_short(wide_ref, taps_ref, 1, at, step)
        two = convolve_short(wide_ref, taps_ref, 2, depth + at, step)
        g = (one * two).astype(bf16).astype(f32)
        g_ref[pl.ds(pl.multiple_of(at * 8, 8 * step), 8 * step), :] = g.reshape(step * 8, LANES)
        decay = decay_ref[...]
        for t in range(step):
            state = decay * state + g[t][None]
        return state

    state = lax.fori_loop(0, rows // step, body, jnp.zeros((MODES, 8, LANES), f32))
    e0_ref[...] = state[:, :4]
    e_ref[...] = reach_ref[:, 4:] * state[:, :4] + state[:, 4:]


def gate(rows, *arrays):
    whole = pl.BlockSpec(memory_space=pltpu.VMEM)
    return pl.pallas_call(
        functools.partial(gate_kernel, rows),
        out_shape=[
            jax.ShapeDtypeStruct((rows * 8, LANES), f32),
            jax.ShapeDtypeStruct((MODES, 4, LANES), f32),
            jax.ShapeDtypeStruct((MODES, 4, LANES), f32),
        ],
        in_specs=[whole] * len(arrays),
        out_specs=[whole] * 3,
        scratch_shapes=[pltpu.VMEM((2 * (rows + HALO) * 8, LANES), f32)],
        compiler_params=params(),
        name="gate",
    )(*arrays)


def convolve_kernel(rows, spot_ref, p_ref, g_ref, e0_ref, ends_ref, taps_ref, decay_ref, gain_ref, reach_ref, chip_ref, bypass_ref, mine_ref, theirs_ref, wide_ref, mod_ref):
    step = 8
    depth = rows + HALO
    core, chip = spot_ref[0], spot_ref[1]
    for half in range(2):
        for tile in range(4):
            val = p_ref[half * rows : half * rows + depth, tile * LANES : (tile + 1) * LANES]
            spread(wide_ref, 0, depth, half, tile, val)

    def earlier(i, state):
        return chip_ref[...] * state + ends_ref[i].astype(f32)

    sin = lax.fori_loop(0, chip, earlier, jnp.zeros((MODES, 4, LANES), f32))
    state = reach_ref[...] * jnp.concatenate([sin, sin], axis=1) + jnp.concatenate(
        [jnp.zeros_like(sin), e0_ref[...]], axis=1
    )
    bypass = bypass_ref[...]

    def body(i, state):
        at = i * step
        put = pl.ds(pl.multiple_of(at * 8, 8 * step), 8 * step)
        g = g_ref[put, :].reshape(step, 8, LANES)
        f0 = convolve_short(wide_ref, taps_ref, 0, at, step)
        decay, gain = decay_ref[...], gain_ref[...]
        rows_out = []
        for t in range(step):
            state = decay * state + g[t][None]
            rows_out.append(f0[t] * (jnp.sum(gain * state, axis=0) + bypass * g[t]))
        mod_ref[put, :] = jnp.concatenate(rows_out, axis=0)
        return state

    lax.fori_loop(0, rows // step, body, state)
    for tile in range(4):
        first = mod_ref[pl.ds(tile, rows, stride=8), :].astype(bf16)
        second = mod_ref[pl.ds(4 + tile, rows, stride=8), :].astype(bf16)
        cols = slice(tile * LANES, (tile + 1) * LANES)
        mine_ref[:, cols] = jnp.where(core == 0, first, second)
        theirs_ref[:, cols] = jnp.where(core == 0, second, first)


def convolve(rows, spot, *arrays):
    whole = pl.BlockSpec(memory_space=pltpu.VMEM)
    return pl.pallas_call(
        functools.partial(convolve_kernel, rows),
        out_shape=[jax.ShapeDtypeStruct((rows, 4 * LANES), bf16)] * 2,
        in_specs=[pl.BlockSpec(memory_space=pltpu.SMEM)] + [whole] * len(arrays),
        out_specs=[whole] * 2,
        scratch_shapes=[
            pltpu.VMEM(((rows + HALO) * 8, LANES), f32),
            pltpu.VMEM((rows * 8, LANES), f32),
        ],
        compiler_params=params(),
        name="convolve",
    )(spot, *arrays)


def output_kernel(count, at_ref, mine_ref, theirs_ref, *refs):
    for a, b, out_ref in zip(refs[:count], refs[count : 2 * count], refs[2 * count :]):
        got = jnp.dot(mine_ref[...], a[...], preferred_element_type=f32)
        got = got + jnp.dot(theirs_ref[...], b[...], preferred_element_type=f32)
        out_ref[...] = got.astype(out_ref.dtype)


def output(core, blocks, mine, theirs, weight, dtypes):
    rows, deep = mine.shape
    count = len(blocks)
    wide = 512
    at = jnp.stack([core] + [jnp.asarray(b, jnp.int32) for b in blocks])
    whole = pl.BlockSpec((rows, deep), lambda i, at: (0, 0))
    in_specs = [whole, whole]
    for other in (False, True):
        for b in range(count):
            in_specs.append(
                pl.BlockSpec(
                    (deep, wide),
                    functools.partial(
                        lambda b, other, i, at: (1 - at[0] if other else at[0], at[1 + b]), b, other
                    ),
                )
            )
    return pl.pallas_call(
        functools.partial(output_kernel, count),
        grid_spec=pltpu.PrefetchScalarGridSpec(
            num_scalar_prefetch=1,
            grid=(1,),
            in_specs=in_specs,
            out_specs=[pl.BlockSpec((rows, wide), lambda i, at: (0, 0))] * count,
        ),
        out_shape=[jax.ShapeDtypeStruct((rows, wide), t) for t in dtypes],
        compiler_params=params(),
        cost_estimate=pl.CostEstimate(
            flops=4 * rows * deep * count * wide, bytes_accessed=0, transcendentals=0
        ),
        name="output",
    )(at, mine, theirs, *([weight] * (2 * count)))


def add_kernel(*refs):
    total = refs[0][...].astype(f32)
    for r in refs[1:-1]:
        total = total + r[...].astype(f32)
    refs[-1][...] = total.astype(bf16)


def add(*arrays):
    whole = pl.BlockSpec(memory_space=pltpu.VMEM)
    return pl.pallas_call(
        add_kernel,
        out_shape=jax.ShapeDtypeStruct(arrays[0].shape, bf16),
        in_specs=[whole] * len(arrays),
        out_specs=whole,
        compiler_params=params(),
        name="add",
    )(*arrays)


def finish_kernel(o0, o1, a0, a1, b0, b1, out_ref):
    half = o0.shape[1]
    for cols, parts in ((slice(0, half), (o0, a0, b0)), (slice(half, None), (o1, a1, b1))):
        total = parts[0][...] + parts[1][...].astype(f32) + parts[2][...].astype(f32)
        out_ref[:, cols] = total.astype(bf16)


def finish(*arrays):
    rows, half = arrays[0].shape
    whole = pl.BlockSpec(memory_space=pltpu.VMEM)
    return pl.pallas_call(
        finish_kernel,
        out_shape=jax.ShapeDtypeStruct((rows, 2 * half), bf16),
        in_specs=[whole] * len(arrays),
        out_specs=whole,
        compiler_params=params(),
        name="finish",
    )(*arrays)


def on_device(tokens, norm_gain, in_weight, short_taps, decay_rates, residues, bypass, out_weight):
    rows = tokens.shape[0]
    chans = in_weight.shape[2]
    half = chans // 2
    quarter = half // 2
    core, z, x, chan = (lax.axis_index(a).astype(jnp.int32) for a in ("core", "z", "x", "chan"))
    nz, nx, ny = (lax.axis_size(a) for a in ("z", "x", "chan"))
    core1 = core.reshape(1)

    def of_core(array, axis, which):
        return lax.dynamic_slice_in_dim(array, which * half, half, axis)

    weight = in_weight.transpose(1, 0, 2)
    weight0 = lax.all_gather(weight[:1], ("z", "x", "core"), axis=1, tiled=True)

    pair = weight[1:]
    kept = of_core(pair, 2, core)
    got = shift(of_core(pair, 2, 1 - core), "core", 1)
    first = jnp.where(core == 0, kept, got)
    second = jnp.where(core == 0, got, kept)
    unit = jnp.concatenate([first, second], axis=1)[None]
    unit_a, unit_b = unit[..., :quarter], unit[..., quarter:]

    other = shift(tokens, "core", 1)
    last = jnp.where(core == 1, tokens[rows - HALO :], other[rows - HALO :])
    halo = from_behind(last, ("z", "x"), 1)
    normed = norm(core1, tokens, other, halo, norm_gain)

    def place(dz, dx):
        return ((z + dz) % nz) * nx + (x + dx) % nx

    b = {0: unit_b}
    b[-1], b[1] = shift(b[0], "z", 1), shift(b[0], "z", -1)
    b[-2], b[2] = shift(b[-1], "z", 1), shift(b[1], "z", -1)
    b[-3], b[3] = shift(b[-2], "z", 1), shift(b[2], "z", -1)
    b[4] = shift(b[3], "z", -1)
    a_m1, a_p1, a_p2 = shift(unit_a, "x", 1), shift(unit_a, "x", -1), shift(unit_a, "x", 2)
    a_order = (0, -1, 1, 2)
    a = {0: join([unit_a, a_m1, a_p1, a_p2])}
    a[-1], a[1] = shift(a[0], "z", 1), shift(a[0], "z", -1)
    a[-2], a[2] = shift(a[-1], "z", 1), shift(a[1], "z", -1)
    a[-3], a[3] = shift(a[-2], "z", 1), shift(a[2], "z", -1)
    a4_low = shift(a[-3][:2], "z", 1)
    a4_high = shift(a[3][2:], "z", -1)

    near, far = (0, -1, 1, 2), (-2, -3, 3, 4)
    b_near = join([b[d] for d in near])
    b_far = join([b[d] for d in far], [normed])
    bn_m1, bn_p1 = shift(b_near, "x", 1), shift(b_near, "x", -1)
    bf_m1, bf_p1 = shift(b_far, "x", 1), shift(b_far, "x", -1)
    bn_p2 = shift(bn_m1, "x", 1)
    bf_p2 = shift(bf_p1, "x", -1)

    def a_places(dz):
        return [place(dz, dx) for dx in a_order]

    acc_a = project(normed, None, [a[0]], a_places(0))
    acc_a = project(normed, acc_a, [a[-1], a[1]], a_places(-1) + a_places(1))
    acc_a = project(normed, acc_a, [a[-2], a[2]], a_places(-2) + a_places(2))
    acc_a = project(
        normed, acc_a, [a[-3], a[3], a4_low, a4_high], a_places(-3) + a_places(3) + a_places(4)
    )

    def b_places(zs, dx):
        return [place(dz, dx) for dz in zs]

    acc_b = project(normed, None, [b_near, b_far], b_places(near, 0) + b_places(far, 0))
    acc_b = project(normed, acc_b, [bn_m1, bn_p1], b_places(near, -1) + b_places(near, 1))
    acc_b = project(
        normed,
        acc_b,
        [bf_m1, bf_p1, bn_p2, bf_p2],
        b_places(far, -1) + b_places(far, 1) + b_places(near, 2) + b_places(far, 2),
    )

    def by_tile(array):
        mine = of_core(array, array.ndim - 1, core)
        tiled = mine.reshape(mine.shape[:-1] + (4, LANES))
        return jnp.concatenate([tiled, tiled], axis=-2)

    rates = by_tile(decay_rates)
    gain = by_tile(residues) * jnp.sqrt(-jnp.expm1(-2.0 * rates))
    decay = jnp.exp(-rates)
    halves = (jnp.arange(8) // 4).astype(f32)[None, :, None]
    reach = jnp.exp(-rates * (halves * float(rows)))
    chip_decay = jnp.exp(-rates[:, :4] * float(2 * rows))
    taps = by_tile(short_taps)

    gated, end_first, end = gate(rows, acc_a, acc_b, taps, decay, reach)

    sent = jnp.broadcast_to(end.reshape(1, MODES, half).astype(bf16), (nz * nx, MODES, half))
    ends = lax.all_to_all(sent, ("z", "x"), 0, 0).reshape(nz * nx, MODES, 4, LANES)
    projected0 = project_all(core1, normed, weight0, half)
    spot = jnp.stack([core, z * nx + x])
    mine, to_swap = convolve(
        rows,
        spot,
        projected0,
        gated,
        end_first,
        ends,
        taps,
        decay,
        gain,
        reach,
        chip_decay,
        by_tile(bypass),
    )
    theirs = shift(to_swap, "core", 1)

    def blocks(dy):
        at = ((chan + dy) % ny) * 2
        return [at, at + 1]

    far0, far1 = output(core, blocks(2), mine, theirs, out_weight, [bf16, bf16])
    next0, next1, prev0, prev1 = output(
        core, blocks(1) + blocks(-1), mine, theirs, out_weight, [f32, bf16, bf16, f32]
    )
    own0, own1 = output(core, blocks(0), mine, theirs, out_weight, [f32, f32])
    via0, via1 = shift(far0, "chan", 1), shift(far1, "chan", -1)
    from_prev1, from_next0 = shift(next1, "chan", 1), shift(prev0, "chan", -1)
    from_prev0 = shift(add(next0, via0), "chan", 1)
    from_next1 = shift(add(prev1, via1), "chan", -1)
    return finish(own0, own1, from_prev0, from_prev1, from_next0, from_next1)


def solution(mesh):
    grid = mesh.devices.reshape(8, 4, 2, 4)
    fine = Mesh(grid, ("z", "x", "core", "chan"))
    seq = ("z", "x", "core")
    in_specs = (
        P(seq, None),
        P(),
        P(seq, None, "chan"),
        P(None, None, "chan"),
        P(None, "chan"),
        P(None, "chan"),
        P("chan"),
        P("chan", None),
    )
    return jax.shard_map(
        on_device, mesh=fine, in_specs=in_specs, out_specs=P(seq, "chan"), check_vma=False
    )
```

time: 973 us -> 229 us (0.24)
  starting transfers between devices: 373 us -> 73.7 us
  waiting for transfers between devices: 312 us -> 61.5 us
  local copies, waits for them, and re-layouts: 110 us -> 8.17 us
  matrix products: 85.6 us -> 0 us
  other arithmetic: 73.3 us -> 2.92 us
  Pallas kernels: 0 us -> 68.4 us
    ppermute x64 -> x34, starting transfers between devices: 373 us -> 63.6 us  [the longest x33 59.6 us: shift(): lax.ppermute(block, axes, [(i, (i + distance) % count) for i in range(cou...]
    reduce_scatter x1 -> x0, waiting for transfers between devices: 140 us -> none  [on_device(): lax.psum_scatter(terms.astype(jnp.bfloat16), 'chan', scatter_dimension=1,...]
    all_gather x1, waiting for transfers between devices: 108 us -> 0.02 us  [on_device(): weight0 = lax.all_gather(weight[:1], ('z', 'x', 'core'), axis=1, tiled=True)]
    dot_general x6 -> x0, matrix products: 85.6 us -> none  [the longest x1 30.9 us: on_device(): inside = jnp.einsum('tsc,isc->itc', toeplitz, blocks, precision=highest)]
    pallas_call x0 -> x20, Pallas kernels: none -> 68.4 us  [the longest x7 26.3 us: project(): pl.pallas_call(functools.partial(project_kernel, counts, acc is not None)...]
    add x71 -> x0, other arithmetic: 57.8 us -> none  [the longest x63 40.3 us: relay(): return (received, device_decay * received + local_end)]
    all_gather x1 -> x0, local copies, waits for them, and re-layouts: 33.3 us -> none  [on_device(): piece = lax.all_gather(in_weight, 'seq', axis=0, tiled=True)]
    dot_general x1 -> x0, local copies, waits for them, and re-layouts: 30.5 us -> none  [on_device(): jnp.einsum('tsk,kc->tsc', selector, filter_taps, precision=highest)]
  transfers between devices with their start and end apart: 66 -> 36, of which waited for: 65 -> 14; matrix products, arithmetic and copies ran while one was open for 8% -> 4% of each run, Pallas kernels for 0% -> 22%
where the time goes in v1:
time: 229 us; the launch traced here: 228 us
  starting transfers between devices  73.7 us (32%)
  Pallas kernels  68.4 us (30%)
  waiting for transfers between devices  61.5 us (27%)
  between operations  13.8 us (6%)
  local copies, waits for them, and re-layouts  8.17 us (4%)
  other arithmetic  2.92 us (1%)
    ppermute x33, starting transfers between devices, shift(): lax.ppermute(block, axes, [(i, (i + distance) % count) for i in range(cou...  59.6 us
    ppermute x33, waiting for transfers between devices, shift(): lax.ppermute(block, axes, [(i, (i + distance) % count) for i in range(cou...  49 us
    pallas_call x7, Pallas kernels, project(): pl.pallas_call(functools.partial(project_kernel, counts, acc is not None)...  26.3 us
    all_to_all x1, waiting for transfers between devices, on_device(): lax.all_to_all(sent, ('z', 'x'), 0, 0).reshape(nz * nx, MODES, 4, LANES)  12.5 us
    pallas_call x3, Pallas kernels, output(): pl.pallas_call(functools.partial(output_kernel, count), grid_spec=pltpu.P...  10.6 us
    all_to_all x1, starting transfers between devices, on_device(): lax.all_to_all(sent, ('z', 'x'), 0, 0).reshape(nz * nx, MODES, 4, LANES)  10.1 us
    pallas_call x1, Pallas kernels, norm(): pl.pallas_call(norm_kernel, out_shape=jax.ShapeDtypeStruct((HALO + 2 * ro...  8.29 us
    pallas_call x1, Pallas kernels, project_all(): pl.pallas_call(project_all_kernel, grid_spec=pltpu.PrefetchScalarGridSpec...  7.28 us
  transfers between devices with their start and end apart: 36, of which 14 were waited for; matrix products, arithmetic and copies ran while one was open for 4% of the time, Pallas kernels for 22%

profile of v1, /device:TPU:1, one launch (start us, length us, event | category | flops | bytes accessed | tf_op | source)
XLA Modules:
  0.0 228.5 jit_solution(7613596935013189452)
XLA Ops:
  8.2 3.3 %collective-permute-start = (bf16[384,4096]{1,0:T(8,128)(2,1)}, bf16[384,4096]{1,0:T(8,128)(2,1)}, u32[]{:S(2)}, u32[]{:S(2)}) collective-permute-start(bf16[384,4096]{1,0:T(8,128)(2,1)} %own_ref.1), channel_id=1, source_target_pairs={{0,4},{4,0},{1,5},{5,1},{2,6},{6,2},{3,7},{7,3},{8,12},{12,8},{9,1... | collective-permute-start | bytes 9437192 | tf_op jit(solution)/shard_map/ppermute | solution.py:21
  13.3 4.0 %collective-permute-done.2 = bf16[2,64,512]{2,1,0:T(8,128)(2,1)} collective-permute-done((bf16[2,64,512]{2,1,0:T(8,128)(2,1)}, bf16[2,64,512]{2,1,0:T(8,128)(2,1)}, u32[]{:S(2)}, u32[]{:S(2)}) %collective-permute-start.2) | collective-permute-done | bytes 131104 | tf_op jit(solution)/shard_map/ppermute | solution.py:21
  21.1 3.2 %collective-permute-done.3.refs_1_ = bf16[1,2,128,256]{3,2,1,0:T(8,128)(2,1)S(1)} collective-permute-done((bf16[1,2,128,256]{3,2,1,0:T(8,128)(2,1)S(1)}, bf16[1,2,128,256]{3,2,1,0:T(8,128)(2,1)S(1)}, u32[]{:S(2)}, u32[]{:S(2)}) %collective-permute-start.3) | collective-permute-done | bytes 131104 | tf_op jit(solution)/shard_map/ppermute | solution.py:21
  28.9 3.9 %collective-permute-start.9 = (bf16[4,2,128,256]{3,2,1,0:T(8,128)(2,1)}, bf16[4,2,128,256]{3,2,1,0:T(8,128)(2,1)}, u32[]{:S(2)}, u32[]{:S(2)}) collective-permute-start(bf16[4,2,128,256]{3,2,1,0:T(8,128)(2,1)} %join.3.refs_4_), channel_id=1, source_target_pairs={{0,224},{32,0},{64,32},{96,64},{128,96},{160,128},{192,160},{224,1... | collective-permute-start | bytes 1572872 | tf_op jit(solution)/shard_map/ppermute | solution.py:21
  34.3 14.4 %collective-permute-done.17.refs_2_ = bf16[1,2,128,256]{3,2,1,0:T(8,128)(2,1)} collective-permute-done((bf16[1,2,128,256]{3,2,1,0:T(8,128)(2,1)S(1)}, bf16[1,2,128,256]{3,2,1,0:T(8,128)(2,1)}, u32[]{:S(2)}, u32[]{:S(2)}) %collective-permute-start.17) | collective-permute-done | bytes 131104 | tf_op jit(solution)/shard_map/ppermute | solution.py:21
  48.6 3.5 %collective-permute-start.18 = (bf16[1,2,128,256]{3,2,1,0:T(8,128)(2,1)}, bf16[1,2,128,256]{3,2,1,0:T(8,128)(2,1)}, u32[]{:S(2)}, u32[]{:S(2)}) collective-permute-start(bf16[1,2,128,256]{3,2,1,0:T(8,128)(2,1)} %collective-permute-done.17.refs_2_), channel_id=1, source_target_pairs={{0,224},{32,0},{64,32},{96,64},{128,96},{160,128},{192,160},{224,1... | collective-permute-start | bytes 393224 | tf_op jit(solution)/shard_map/ppermute | solution.py:21
  54.6 3.1 %collective-permute-start.19 = (bf16[1,2,128,256]{3,2,1,0:T(8,128)(2,1)}, bf16[1,2,128,256]{3,2,1,0:T(8,128)(2,1)}, u32[]{:S(2)}, u32[]{:S(2)}) collective-permute-start(bf16[1,2,128,256]{3,2,1,0:T(8,128)(2,1)} %collective-permute-done.18.refs_3_), channel_id=1, source_target_pairs={{0,224},{32,0},{64,32},{96,64},{128,96},{160,128},{192,160},{224,1... | collective-permute-start | bytes 393224 | tf_op jit(solution)/shard_map/ppermute | solution.py:21
  61.9 4.0 %collective-permute-start.1 = (bf16[16,4096]{1,0:T(8,128)(2,1)}, bf16[16,4096]{1,0:T(8,128)(2,1)}, u32[]{:S(2)}, u32[]{:S(2)}) collective-permute-start(bf16[16,4096]{1,0:T(8,128)(2,1)} %slice_select_fusion), channel_id=1, source_target_pairs={{0,8},{8,16},{16,24},{24,32},{32,40},{40,48},{48,56},{56,64},{64,7... | collective-permute-start | bytes 393224 | tf_op jit(solution)/shard_map/ppermute | solution.py:26
  72.7 8.3 %norm.1.left_ref.refs_0_.refs_1_.refs_2_.refs_3_.refs_4_.refs_5_.refs_6_.refs_7_.refs_8_.refs_9_.refs_10_.refs_11_.refs_12_.refs_13_.refs_14_.refs_15_ = bf16[784,4096]{1,0:T(8,128)(2,1)} custom-call(s32[1]{0:T(128)} %bitcast.core_ref, bf16[384,4096]{1,0:T(8,128)(2,1)S(1)} %copy-done.1, bf16[384,4096]{1,0:T(8,128)(2,1)} %collective-permute-done.other_ref, ...), custom_call_target="tpu_custom_call" | custom-call | tf_op jit(solution)/shard_map/norm/pallas_call | solution.py:60
  92.7 6.0 %collective-permute-done.8.refs_12_ = bf16[4,2,128,256]{3,2,1,0:T(8,128)(2,1)} collective-permute-done((bf16[4,2,128,256]{3,2,1,0:T(8,128)(2,1)}, bf16[4,2,128,256]{3,2,1,0:T(8,128)(2,1)}, u32[]{:S(2)}, u32[]{:S(2)}) %collective-permute-start.8) | collective-permute-done | bytes 524320 | tf_op jit(solution)/shard_map/ppermute | solution.py:21
  103.1 3.5 %project.11.refs_10_ = f32[2,784,256]{2,1,0:T(8,128)S(1)} custom-call(s32[8]{0:T(128)S(1)} %stack.238.offs_ref, bf16[784,4096]{1,0:T(8,128)(2,1)} %norm.1.left_ref.refs_0_.refs_1_.refs_2_.refs_3_.refs_4_.refs_5_.refs_6_.refs_7_.refs_8_.refs_9_.refs_10_.refs_11_.refs_12_.refs_13_.refs_14_.refs_15_, ...), custom_call_target="tpu_custom_call" | custom-call | flops 822083584 | bytes 3211264 | tf_op jit(solution)/shard_map/project/pallas_call | solution.py:107
  111.7 3.6 %project.8.refs_10_ = f32[2,784,256]{2,1,0:T(8,128)S(1)} custom-call(s32[8]{0:T(128)S(1)} %stack.230.offs_ref, bf16[784,4096]{1,0:T(8,128)(2,1)} %norm.1.left_ref.refs_0_.refs_1_.refs_2_.refs_3_.refs_4_.refs_5_.refs_6_.refs_7_.refs_8_.refs_9_.refs_10_.refs_11_.refs_12_.refs_13_.refs_14_.refs_15_, ...), custom_call_target="tpu_custom_call", output_to_operand_aliasing={{}: (11, {})} | custom-call | flops 822083584 | bytes 3211264 | tf_op jit(solution)/shard_map/project/pallas_call | solution.py:107
  115.2 3.6 %project.9.refs_16_ = f32[2,784,256]{2,1,0:T(8,128)S(1)} custom-call(s32[8]{0:T(128)S(1)} %stack.221.offs_ref, bf16[784,4096]{1,0:T(8,128)(2,1)} %norm.1.left_ref.refs_0_.refs_1_.refs_2_.refs_3_.refs_4_.refs_5_.refs_6_.refs_7_.refs_8_.refs_9_.refs_10_.refs_11_.refs_12_.refs_13_.refs_14_.refs_15_, ...), custom_call_target="tpu_custom_call", output_to_operand_aliasing={{}: (11, {})} | custom-call | flops 822083584 | bytes 3211264 | tf_op jit(solution)/shard_map/project/pallas_call | solution.py:107
  118.8 3.6 %project.12.refs_20_ = f32[2,784,256]{2,1,0:T(8,128)S(1)} custom-call(s32[8]{0:T(128)S(1)} %stack.237.offs_ref, bf16[784,4096]{1,0:T(8,128)(2,1)} %norm.1.left_ref.refs_0_.refs_1_.refs_2_.refs_3_.refs_4_.refs_5_.refs_6_.refs_7_.refs_8_.refs_9_.refs_10_.refs_11_.refs_12_.refs_13_.refs_14_.refs_15_, ...), custom_call_target="tpu_custom_call", output_to_operand_aliasing={{}: (11, {})} | custom-call | flops 822083584 | bytes 3211264 | tf_op jit(solution)/shard_map/project/pallas_call | solution.py:107
  122.4 4.3 %project.10.a_ref = f32[2,784,256]{2,1,0:T(8,128)S(1)} custom-call(s32[12]{0:T(128)S(1)} %stack.212.offs_ref, bf16[784,4096]{1,0:T(8,128)(2,1)} %norm.1.left_ref.refs_0_.refs_1_.refs_2_.refs_3_.refs_4_.refs_5_.refs_6_.refs_7_.refs_8_.refs_9_.refs_10_.refs_11_.refs_12_.refs_13_.refs_14_.refs_15_, ...), custom_call_target="tpu_custom_call", output_to_operand_aliasing={{}: (17, {})} | custom-call | flops 1233125376 | bytes 3211264 | tf_op jit(solution)/shard_map/project/pallas_call | solution.py:107
  126.8 5.2 %project.13.b_ref = f32[2,784,256]{2,1,0:T(8,128)S(1)} custom-call(s32[16]{0:T(128)S(1)} %stack.236.offs_ref, bf16[784,4096]{1,0:T(8,128)(2,1)} %norm.1.left_ref.refs_0_.refs_1_.refs_2_.refs_3_.refs_4_.refs_5_.refs_6_.refs_7_.refs_8_.refs_9_.refs_10_.refs_11_.refs_12_.refs_13_.refs_14_.refs_15_, ...), custom_call_target="tpu_custom_call", output_to_operand_aliasing={{}: (21, {})} | custom-call | flops 1644167168 | bytes 3211264 | tf_op jit(solution)/shard_map/project/pallas_call | solution.py:107
  131.9 4.6 %gate.1 = (f32[3072,128]{1,0:T(8,128)S(1)}, f32[16,4,128]{2,1,0:T(4,128)S(1)}, f32[16,4,128]{2,1,0:T(4,128)S(1)}) custom-call(f32[2,784,256]{2,1,0:T(8,128)S(1)} %project.10.a_ref, f32[2,784,256]{2,1,0:T(8,128)S(1)} %project.13.b_ref, f32[3,7,8,128]{3,2,1,0:T(8,128)S(1)} %pad_maximum_fusion.taps_ref, f32[16,8,128]{2,1,0:T(8,128)S(1)} %get-tuple-element.37.decay_ref, ...), custom_call_target="tpu_custom_call" | custom-call | tf_op jit(solution)/shard_map/gate/pallas_call | solution.py:211
  137.5 10.1 %all-to-all-start = ((bf16[32,16,512]{2,1,0:T(8,128)(2,1)}), bf16[32,16,512]{2,1,0:T(8,128)(2,1)S(1)}, u32[]{:S(2)}, u32[]{:S(2)}) async-start(bf16[32,16,512]{2,1,0:T(8,128)(2,1)} %broadcast_in_dim.10), calls=%async_computation | async-start | bytes 1048576 | tf_op jit(solution)/shard_map/all_to_all | solution.py:453
  147.8 12.5 %all-to-all-done = bf16[32,16,512]{2,1,0:T(8,128)(2,1)S(1)} async-done(((bf16[32,16,512]{2,1,0:T(8,128)(2,1)}), bf16[32,16,512]{2,1,0:T(8,128)(2,1)S(1)}, u32[]{:S(2)}, u32[]{:S(2)}) %all-to-all-start) | async-done | bytes 524320 | tf_op jit(solution)/shard_map/all_to_all | solution.py:453
  160.5 7.3 %project_all.1.p_ref = f32[784,512]{1,0:T(8,128)S(1)} custom-call(s32[1]{0:T(128)} %bitcast.core_ref, bf16[784,4096]{1,0:T(8,128)(2,1)} %norm.1.left_ref.refs_0_.refs_1_.refs_2_.refs_3_.refs_4_.refs_5_.refs_6_.refs_7_.refs_8_.refs_9_.refs_10_.refs_11_.refs_12_.refs_13_.refs_14_.refs_15_, bf16[1,4096,1024]{2,1,0:T(8,128)(2,1)} %all-gather.2.cloned.1.call-done.right_ref), custom_call_target="tpu_custom_call" | custom-call | flops 3288334336 | bytes 6422528 | tf_op jit(solution)/shard_map/project_all/pallas_call | solution.py:147
  167.7 6.1 %convolve.1 = (bf16[384,512]{1,0:T(8,128)(2,1)S(1)}, bf16[384,512]{1,0:T(8,128)(2,1)S(1)}) custom-call(s32[2]{0:T(128)S(1)} %pad_add_fusion.1.spot_ref, f32[784,512]{1,0:T(8,128)S(1)} %project_all.1.p_ref, f32[3072,128]{1,0:T(8,128)S(1)} %get-tuple-element.18.g_ref, f32[16,4,128]{2,1,0:T(4,128)S(1)} %get-tuple-element.19.e0_ref, ...), custom_call_target="tpu_custom_call" | custom-call | tf_op jit(solution)/shard_map/convolve/pallas_call | solution.py:268
  173.9 13.1 %collective-permute-start.27 = (bf16[384,512]{1,0:T(8,128)(2,1)S(1)}, bf16[384,512]{1,0:T(8,128)(2,1)S(1)}, u32[]{:S(2)}, u32[]{:S(2)}) collective-permute-start(bf16[384,512]{1,0:T(8,128)(2,1)S(1)} %get-tuple-element.22), channel_id=1, source_target_pairs={{0,4},{4,0},{1,5},{5,1},{2,6},{6,2},{3,7},{7,3},{8,12},{12,8},{9,1... | collective-permute-start | bytes 1179656 | tf_op jit(solution)/shard_map/ppermute | solution.py:21
  194.7 4.5 %output.4 = (f32[384,512]{1,0:T(8,128)S(1)}, bf16[384,512]{1,0:T(8,128)(2,1)S(1)}, bf16[384,512]{1,0:T(8,128)(2,1)S(1)}, f32[384,512]{1,0:T(8,128)S(1)}) custom-call(s32[5]{0:T(128)S(1)} %stack.243.at_ref, bf16[384,512]{1,0:T(8,128)(2,1)S(1)} %get-tuple-element.21.mine_ref, bf16[384,512]{1,0:T(8,128)(2,1)S(1)} %collective-permute-done.27.theirs_ref, ...), custom_call_target="tpu_custom_call" | custom-call | flops 1610612736 | tf_op jit(solution)/shard_map/output/pallas_call | solution.py:306
  212.1 8.4 %collective-permute-done.29.a0 = bf16[384,512]{1,0:T(8,128)(2,1)S(1)} collective-permute-done((bf16[384,512]{1,0:T(8,128)(2,1)S(1)}, bf16[384,512]{1,0:T(8,128)(2,1)S(1)}, u32[]{:S(2)}, u32[]{:S(2)}) %collective-permute-start.29) | collective-permute-done | bytes 393248 | tf_op jit(solution)/shard_map/ppermute | solution.py:21
  (117 shorter events, 70.5 us)
Async XLA Ops:
  6.5 153.9 %all-gather.2.cloned.1.call-start = ((), (), s32[]{:S(2)}) async-start(), calls=%async_computation.1 | async-start | bytes 8519680 | tf_op jit(solution)/shard_map/all_gather | solution.py:375
  8.2 52.2 %collective-permute-start = (bf16[384,4096]{1,0:T(8,128)(2,1)}, bf16[384,4096]{1,0:T(8,128)(2,1)}, u32[]{:S(2)}, u32[]{:S(2)}) collective-permute-start(bf16[384,4096]{1,0:T(8,128)(2,1)} %own_ref.1), channel_id=1, source_target_pairs={{0,4},{4,0},{1,5},{5,1},{2,6},{6,2},{3,7},{7,3},{8,12},{12,8},{9,1... | collective-permute-start | bytes 9437192 | tf_op jit(solution)/shard_map/ppermute | solution.py:21
  27.2 30.4 %collective-permute-start.6 = (bf16[4,2,128,256]{3,2,1,0:T(8,128)(2,1)}, bf16[4,2,128,256]{3,2,1,0:T(8,128)(2,1)}, u32[]{:S(2)}, u32[]{:S(2)}) collective-permute-start(bf16[4,2,128,256]{3,2,1,0:T(8,128)(2,1)} %join.3.refs_4_), channel_id=1, source_target_pairs={{0,32},{32,64},{64,96},{96,128},{128,160},{160,192},{192,224},{224... | collective-permute-start | bytes 1572872 | tf_op jit(solution)/shard_map/ppermute | solution.py:21
  28.9 28.8 %collective-permute-start.9 = (bf16[4,2,128,256]{3,2,1,0:T(8,128)(2,1)}, bf16[4,2,128,256]{3,2,1,0:T(8,128)(2,1)}, u32[]{:S(2)}, u32[]{:S(2)}) collective-permute-start(bf16[4,2,128,256]{3,2,1,0:T(8,128)(2,1)} %join.3.refs_4_), channel_id=1, source_target_pairs={{0,224},{32,0},{64,32},{96,64},{128,96},{160,128},{192,160},{224,1... | collective-permute-start | bytes 1572872 | tf_op jit(solution)/shard_map/ppermute | solution.py:21
  32.8 15.8 %collective-permute-start.17 = (bf16[1,2,128,256]{3,2,1,0:T(8,128)(2,1)S(1)}, bf16[1,2,128,256]{3,2,1,0:T(8,128)(2,1)}, u32[]{:S(2)}, u32[]{:S(2)}) collective-permute-start(bf16[1,2,128,256]{3,2,1,0:T(8,128)(2,1)S(1)} %get-tuple-element.33.refs_0_), channel_id=1, source_target_pairs={{0,224},{32,0},{64,32},{96,64},{128,96},{160,128},{192,160},{224,1... | collective-permute-start | bytes 393224 | tf_op jit(solution)/shard_map/ppermute | solution.py:21
  34.3 17.9 %collective-permute-start.14 = (bf16[1,2,128,256]{3,2,1,0:T(8,128)(2,1)S(1)}, bf16[1,2,128,256]{3,2,1,0:T(8,128)(2,1)}, u32[]{:S(2)}, u32[]{:S(2)}) collective-permute-start(bf16[1,2,128,256]{3,2,1,0:T(8,128)(2,1)S(1)} %get-tuple-element.33.refs_0_), channel_id=1, source_target_pairs={{0,32},{32,64},{64,96},{96,128},{128,160},{160,192},{192,224},{224... | collective-permute-start | bytes 393224 | tf_op jit(solution)/shard_map/ppermute | solution.py:21
  57.7 14.9 %collective-permute-start.7 = (bf16[4,2,128,256]{3,2,1,0:T(8,128)(2,1)}, bf16[4,2,128,256]{3,2,1,0:T(8,128)(2,1)}, u32[]{:S(2)}, u32[]{:S(2)}) collective-permute-start(bf16[4,2,128,256]{3,2,1,0:T(8,128)(2,1)} %collective-permute-done.6.refs_8_), channel_id=1, source_target_pairs={{0,32},{32,64},{64,96},{96,128},{128,160},{160,192},{192,224},{224... | collective-permute-start | bytes 1572872 | tf_op jit(solution)/shard_map/ppermute | solution.py:21
  57.7 27.7 %collective-permute-start.10 = (bf16[4,2,128,256]{3,2,1,0:T(8,128)(2,1)}, bf16[4,2,128,256]{3,2,1,0:T(8,128)(2,1)}, u32[]{:S(2)}, u32[]{:S(2)}) collective-permute-start(bf16[4,2,128,256]{3,2,1,0:T(8,128)(2,1)} %collective-permute-done.9.refs_9_), channel_id=1, source_target_pairs={{0,224},{32,0},{64,32},{96,64},{128,96},{160,128},{192,160},{224,1... | collective-permute-start | bytes 1572872 | tf_op jit(solution)/shard_map/ppermute | solution.py:21
  65.9 15.1 %collective-permute-start.16 = (bf16[1,2,128,256]{3,2,1,0:T(8,128)(2,1)S(1)}, bf16[1,2,128,256]{3,2,1,0:T(8,128)(2,1)}, u32[]{:S(2)}, u32[]{:S(2)}) collective-permute-start(bf16[1,2,128,256]{3,2,1,0:T(8,128)(2,1)S(1)} %collective-permute-done.15.refs_0_), channel_id=1, source_target_pairs={{0,32},{32,64},{64,96},{96,128},{128,160},{160,192},{192,224},{224... | collective-permute-start | bytes 393224 | tf_op jit(solution)/shard_map/ppermute | solution.py:21
  66.0 16.0 %collective-permute-start.20 = (bf16[1,2,128,256]{3,2,1,0:T(8,128)(2,1)}, bf16[1,2,128,256]{3,2,1,0:T(8,128)(2,1)}, u32[]{:S(2)}, u32[]{:S(2)}) collective-permute-start(bf16[1,2,128,256]{3,2,1,0:T(8,128)(2,1)} %collective-permute-done.19.refs_2_), channel_id=1, source_target_pairs={{0,224},{32,0},{64,32},{96,64},{128,96},{160,128},{192,160},{224,1... | collective-permute-start | bytes 393224 | tf_op jit(solution)/shard_map/ppermute | solution.py:21
  72.6 17.9 %collective-permute-start.23 = (bf16[4,2,128,256]{3,2,1,0:T(8,128)(2,1)}, bf16[4,2,128,256]{3,2,1,0:T(8,128)(2,1)}, u32[]{:S(2)}, u32[]{:S(2)}) collective-permute-start(bf16[4,2,128,256]{3,2,1,0:T(8,128)(2,1)} %join.5.refs_8_), channel_id=1, source_target_pairs={{0,8},{8,16},{16,24},{24,0},{1,9},{9,17},{17,25},{25,1},{2,10},{10... | collective-permute-start | bytes 1572872 | tf_op jit(solution)/shard_map/ppermute | solution.py:21
  72.6 26.1 %collective-permute-start.8 = (bf16[4,2,128,256]{3,2,1,0:T(8,128)(2,1)}, bf16[4,2,128,256]{3,2,1,0:T(8,128)(2,1)}, u32[]{:S(2)}, u32[]{:S(2)}) collective-permute-start(bf16[4,2,128,256]{3,2,1,0:T(8,128)(2,1)} %collective-permute-done.7.refs_8_), channel_id=1, source_target_pairs={{0,32},{32,64},{64,96},{96,128},{128,160},{160,192},{192,224},{224... | collective-permute-start | bytes 1572872 | tf_op jit(solution)/shard_map/ppermute | solution.py:21
  83.0 16.2 %collective-permute-start.22 = (bf16[4,2,128,256]{3,2,1,0:T(8,128)(2,1)S(1)}, bf16[4,2,128,256]{3,2,1,0:T(8,128)(2,1)S(1)}, u32[]{:S(2)}, u32[]{:S(2)}) collective-permute-start(bf16[4,2,128,256]{3,2,1,0:T(8,128)(2,1)S(1)} %join.4.refs_9_), channel_id=1, source_target_pairs={{0,24},{8,0},{16,8},{24,16},{1,25},{9,1},{17,9},{25,17},{2,26},{10... | collective-permute-start | bytes 1572872 | tf_op jit(solution)/shard_map/ppermute | solution.py:21
  85.4 17.0 %collective-permute-start.11 = (bf16[4,2,128,256]{3,2,1,0:T(8,128)(2,1)}, bf16[4,2,128,256]{3,2,1,0:T(8,128)(2,1)S(1)}, u32[]{:S(2)}, u32[]{:S(2)}) collective-permute-start(bf16[4,2,128,256]{3,2,1,0:T(8,128)(2,1)} %collective-permute-done.10.refs_9_), channel_id=1, source_target_pairs={{0,224},{32,0},{64,32},{96,64},{128,96},{160,128},{192,160},{224,1... | collective-permute-start | bytes 1572872 | tf_op jit(solution)/shard_map/ppermute | solution.py:21
  88.2 18.5 %collective-permute-start.26 = (bf16[4,2,128,256]{3,2,1,0:T(8,128)(2,1)}, bf16[4,2,128,256]{3,2,1,0:T(8,128)(2,1)S(1)}, u32[]{:S(2)}, u32[]{:S(2)}) collective-permute-start(bf16[4,2,128,256]{3,2,1,0:T(8,128)(2,1)} %join.5.refs_8_), channel_id=1, source_target_pairs={{0,24},{8,0},{16,8},{24,16},{1,25},{9,1},{17,9},{25,17},{2,26},{10... | collective-permute-start | bytes 1572872 | tf_op jit(solution)/shard_map/ppermute | solution.py:21
  90.5 36.2 %collective-permute-start.24 = (bf16[4,2,128,256]{3,2,1,0:T(8,128)(2,1)}, bf16[4,2,128,256]{3,2,1,0:T(8,128)(2,1)S(1)}, u32[]{:S(2)}, u32[]{:S(2)}) collective-permute-start(bf16[4,2,128,256]{3,2,1,0:T(8,128)(2,1)} %collective-permute-done.23.refs_8_), channel_id=1, source_target_pairs={{0,8},{8,16},{16,24},{24,0},{1,9},{9,17},{17,25},{25,1},{2,10},{10... | collective-permute-start | bytes 1572872 | tf_op jit(solution)/shard_map/ppermute | solution.py:21
  98.7 28.1 %collective-permute-start.21 = (bf16[4,2,128,256]{3,2,1,0:T(8,128)(2,1)S(1)}, bf16[4,2,128,256]{3,2,1,0:T(8,128)(2,1)S(1)}, u32[]{:S(2)}, u32[]{:S(2)}) collective-permute-start(bf16[4,2,128,256]{3,2,1,0:T(8,128)(2,1)S(1)} %join.4.refs_9_), channel_id=1, source_target_pairs={{0,8},{8,16},{16,24},{24,0},{1,9},{9,17},{17,25},{25,1},{2,10},{10... | collective-permute-start | bytes 1572872 | tf_op jit(solution)/shard_map/ppermute | solution.py:21
  99.2 27.5 %collective-permute-start.25 = (bf16[4,2,128,256]{3,2,1,0:T(8,128)(2,1)S(1)}, bf16[4,2,128,256]{3,2,1,0:T(8,128)(2,1)S(1)}, u32[]{:S(2)}, u32[]{:S(2)}) collective-permute-start(bf16[4,2,128,256]{3,2,1,0:T(8,128)(2,1)S(1)} %collective-permute-done.22.refs_17_), channel_id=1, source_target_pairs={{0,24},{8,0},{16,8},{24,16},{1,25},{9,1},{17,9},{25,17},{2,26},{10... | collective-permute-start | bytes 1572872 | tf_op jit(solution)/shard_map/ppermute | solution.py:21
  102.4 19.9 %collective-permute-start.12 = (bf16[2,2,128,256]{3,2,1,0:T(8,128)(2,1)S(1)}, bf16[2,2,128,256]{3,2,1,0:T(8,128)(2,1)S(1)}, u32[]{:S(2)}, u32[]{:S(2)}) collective-permute-start(bf16[2,2,128,256]{3,2,1,0:T(8,128)(2,1)S(1)} %slice.36), channel_id=1, source_target_pairs={{0,32},{32,64},{64,96},{96,128},{128,160},{160,192},{192,224},{224... | collective-permute-start | bytes 786440 | tf_op jit(solution)/shard_map/ppermute | solution.py:21
  106.6 15.7 %collective-permute-start.13 = (bf16[2,2,128,256]{3,2,1,0:T(8,128)(2,1)S(1)}, bf16[2,2,128,256]{3,2,1,0:T(8,128)(2,1)S(1)}, u32[]{:S(2)}, u32[]{:S(2)}) collective-permute-start(bf16[2,2,128,256]{3,2,1,0:T(8,128)(2,1)S(1)} %slice.37), channel_id=1, source_target_pairs={{0,224},{32,0},{64,32},{96,64},{128,96},{160,128},{192,160},{224,1... | collective-permute-start | bytes 786440 | tf_op jit(solution)/shard_map/ppermute | solution.py:21
  137.5 22.8 %all-to-all-start = ((bf16[32,16,512]{2,1,0:T(8,128)(2,1)}), bf16[32,16,512]{2,1,0:T(8,128)(2,1)S(1)}, u32[]{:S(2)}, u32[]{:S(2)}) async-start(bf16[32,16,512]{2,1,0:T(8,128)(2,1)} %broadcast_in_dim.10), calls=%async_computation | async-start | bytes 1048576 | tf_op jit(solution)/shard_map/all_to_all | solution.py:453
  173.9 14.5 %collective-permute-start.27 = (bf16[384,512]{1,0:T(8,128)(2,1)S(1)}, bf16[384,512]{1,0:T(8,128)(2,1)S(1)}, u32[]{:S(2)}, u32[]{:S(2)}) collective-permute-start(bf16[384,512]{1,0:T(8,128)(2,1)S(1)} %get-tuple-element.22), channel_id=1, source_target_pairs={{0,4},{4,0},{1,5},{5,1},{2,6},{6,2},{3,7},{7,3},{8,12},{12,8},{9,1... | collective-permute-start | bytes 1179656 | tf_op jit(solution)/shard_map/ppermute | solution.py:21
  203.7 16.8 %collective-permute-start.29 = (bf16[384,512]{1,0:T(8,128)(2,1)S(1)}, bf16[384,512]{1,0:T(8,128)(2,1)S(1)}, u32[]{:S(2)}, u32[]{:S(2)}) collective-permute-start(bf16[384,512]{1,0:T(8,128)(2,1)S(1)} %add.542), channel_id=1, source_target_pairs={{0,1},{1,2},{2,3},{3,0},{4,5},{5,6},{6,7},{7,4},{8,9},{9,10},{10,1... | collective-permute-start | bytes 1179656 | tf_op jit(solution)/shard_map/ppermute | solution.py:21
  203.9 16.6 %collective-permute-start.33 = (bf16[384,512]{1,0:T(8,128)(2,1)S(1)}, bf16[384,512]{1,0:T(8,128)(2,1)S(1)}, u32[]{:S(2)}, u32[]{:S(2)}) collective-permute-start(bf16[384,512]{1,0:T(8,128)(2,1)S(1)} %add.543), channel_id=1, source_target_pairs={{0,3},{1,0},{2,1},{3,2},{4,7},{5,4},{6,5},{7,6},{8,11},{9,8},{10,9... | collective-permute-start | bytes 1179656 | tf_op jit(solution)/shard_map/ppermute | solution.py:21
  (19 other events, 305.1 us)
Sparse Core Ops, SparseCore 0:
  10.1 96.8 all-gather.1
